TPU v7x, 512 devices: a whole 4x8x8 slice. The times are simulated.
512 devices in a mesh: dp: 64 (over x, y, core), shard: 8 (over z).
Axes of the slice: x: 4, y: 8, z: 8, core: 2. Of those that a mesh axis runs over, the one named last changes fastest.
Arguments:
- layer_input: bfloat16 [49152, 3968], P('dp', 'shard'), may hold values from -6 to 6
- output_grad: bfloat16 [49152, 1984], P('dp', 'shard'), may hold values from -0.21875 to 0.21875
- error_buffer: bfloat16 [64, 3968, 1984], P('dp', 'shard'), may hold values from -4 to 4
- q_start: float32 [1984, 32], P('shard'), may hold values from -6 to 6
Outputs:
- new_error: bfloat16 [64, 3968, 1984], P('dp', 'shard')
- q_factor: float32 [1984, 32], P('shard')
All inputs are finite; a program needn't handle non-finite values.
Results may differ from a plain program's by a relative error of at most 0.0075.
Values may be sent and summed in bfloat16 or wider, within the bound.
A program may use at most 64 MiB of HBM per device.

v0:
```python
import jax
import jax.numpy as jnp
from jax import lax
from jax.sharding import PartitionSpec as P


def on_device(layer_input, output_grad, error_buffer, q_start):
    workers = lax.axis_size("dp")
    gradient = lax.dot_general(
        layer_input,
        lax.all_gather(output_grad, "shard", axis=1, tiled=True),
        (((0,), (0,)), ((), ())),
        preferred_element_type=jnp.float32,
    )
    merged = gradient + error_buffer[0].astype(jnp.float32)
    start_full = lax.all_gather(q_start, "shard", axis=0, tiled=True)
    left_part = jnp.dot(merged, start_full, precision=lax.Precision.HIGHEST)
    p_sum = lax.psum(left_part, "dp")
    gram = lax.psum(jnp.dot(p_sum.T, p_sum, precision=lax.Precision.HIGHEST), "shard")
    lower = jnp.linalg.cholesky(gram)
    p_hat = jax.scipy.linalg.solve_triangular(lower, p_sum.T, lower=True).T
    right_part = (
        lax.dot_general(merged, p_hat, (((0,), (0,)), ((), ())), precision=lax.Precision.HIGHEST)
        / workers
    )
    own_rows = q_start.shape[0]
    right_full = lax.psum(right_part, ("dp", "shard"))
    right_own = lax.dynamic_slice_in_dim(
        right_full, lax.axis_index("shard") * own_rows, own_rows, 0
    )
    approx = jnp.dot(p_hat, right_full.T, precision=lax.Precision.HIGHEST)
    new_error = (merged - approx).astype(jnp.bfloat16)[None]
    return (new_error, right_own)


def solution(mesh):
    return jax.shard_map(
        on_device,
        mesh=mesh,
        in_specs=(P("dp", "shard"), P("dp", "shard"), P("dp", "shard", None), P("shard", None)),
        out_specs=(P("dp", "shard", None), P("shard", None)),
        check_vma=False,
    )
```

profile of v0, /device:TPU:1, one launch (start us, length us, event | category | flops | bytes accessed | tf_op | source)
XLA Modules:
  0.0 638.7 jit_solution(64877079270114391)
XLA Ops:
  7.2 0.0 copy-start
  7.2 0.0 all-gather.3.cloned.1.call-start
  7.2 0.7 all-gather.3.cloned.1.call-update
  7.9 0.0 all-reduce.2.cloned.1.call-start
  8.0 26.3 %all-gather = f32[8,248,32]{1,2,0:T(8,128)S(1)} all-gather(f32[1,248,32]{1,2,0:T(8,128)} %bitcast.28), channel_id=1, replica_groups=mesh['dp'=64,'shard'=8] {'shard'}, dimensions={0}, use_global_device_ids=true | all-gather | bytes 285696 | tf_op jit(solution)/shard_map/all_gather | solution.py:16
  34.3 0.2 copy.11
  34.4 0.1 reshape.18
  34.6 29.0 %all-gather.3.cloned.1.call-done = bf16[768,1984]{0,1:T(8,128)(2,1)} async-done(((bf16[768,248]{0,1:T(8,128)(2,1)}), bf16[768,1984]{0,1:T(8,128)(2,1)}) %all-gather.3.cloned.1.call-update) | async-done | bytes 3047440 | tf_op jit(solution)/shard_map/all_gather | solution.py:11
  63.6 0.0 copy-done
  63.6 4.3 convert_add_fusion
  67.8 0.0 copy-start.1
  67.8 1.9 copy-done.1
  69.7 3.6 fusion.5
  73.3 245.7 %psum.21 = f32[496,32]{0,1:T(8,128)S(1)} all-reduce(f32[496,32]{0,1:T(8,128)S(1)} %fusion.5), channel_id=1, replica_groups=mesh['dp'=64,'shard'=8] {'dp'}, use_global_device_ids=true, to_apply=%region_0.0 | all-reduce | flops 15872 | bytes 126976 | tf_op jit(solution)/shard_map/psum | solution.py:18
  319.0 0.2 fusion.6
  319.2 21.6 %psum.22 = f32[32,32]{0,1:T(8,128)S(1)} all-reduce(f32[32,32]{0,1:T(8,128)S(1)} %fusion.6), channel_id=1, replica_groups=mesh['dp'=64,'shard'=8] {'shard'}, use_global_device_ids=true, to_apply=%region_1.0 | all-reduce | flops 1024 | bytes 8192 | tf_op jit(solution)/shard_map/psum | solution.py:19
  340.8 0.1 copy.13
  340.9 2.9 cholesky.16
  343.8 0.6 compare_reduce_fusion
  344.5 0.7 fusion.1
  345.1 2.4 custom-call.7
  347.5 0.3 fusion.2
  347.8 5.4 convolution_multiply_fusion
  353.2 0.0 all-reduce.2.cloned.1.call-update
  353.3 270.8 %all-reduce.2.cloned.1.call-done = f32[1984,32]{0,1:T(8,128)} async-done(((f32[1984,32]{0,1:T(8,128)}), f32[1984,32]{0,1:T(8,128)}) %all-reduce.2.cloned.1.call-update) | async-done | bytes 253968 | tf_op jit(solution)/shard_map/psum | solution.py:27
  624.1 6.3 fusion
  630.4 1.5 constant_dynamic-slice_fusion
  (2 shorter events, 0.0 us)
Async XLA Ops:
  7.2 56.4 %copy-start = (bf16[768,496]{0,1:T(8,128)(2,1)S(1)}, bf16[768,496]{0,1:T(8,128)(2,1)}, u32[]{:S(2)}) copy-start(bf16[768,496]{0,1:T(8,128)(2,1)} %param.4) | copy-start | bytes 2285572
  7.2 56.4 %all-gather.3.cloned.1.call-start = ((), (), s32[]{:S(2)}) async-start(), calls=%async_computation | async-start | bytes 3428352 | tf_op jit(solution)/shard_map/all_gather | solution.py:11
  7.9 616.2 %all-reduce.2.cloned.1.call-start = ((), (), s32[]{:S(2)}) async-start(), calls=%async_computation.1 | async-start | bytes 524288 | tf_op jit(solution)/shard_map/psum | solution.py:27
  67.8 1.9 copy-start.1
Sparse Core Ops, SparseCore 0:
  10.1 53.4 all-gather.2
  353.4 270.6 all-reduce.1
where the time goes:
time: 639 us
  waiting for transfers between devices  300 us (47%)
  blocking collectives  294 us (46%)
  matrix products  20 us (3%)
  between operations  14.1 us (2%)
  other arithmetic  6.69 us (1%)
    psum x1, waiting for transfers between devices, on_device(): right_full = lax.psum(right_part, ('dp', 'shard'))  271 us
    psum x1, blocking collectives, on_device(): p_sum = lax.psum(left_part, 'dp')  246 us
    all_gather x1, waiting for transfers between devices, on_device(): lax.all_gather(output_grad, 'shard', axis=1, tiled=True)  29 us
    all_gather x1, blocking collectives, on_device(): start_full = lax.all_gather(q_start, 'shard', axis=0, tiled=True)  26.3 us
    psum x1, blocking collectives, on_device(): lax.psum(jnp.dot(p_sum.T, p_sum, precision=lax.Precision.HIGHEST), 'shard')  21.6 us
  transfers between devices with their start and end apart: 2, of which 2 were waited for; matrix products, arithmetic and copies ran while one was open for 0% of the time, Pallas kernels for 0%

commit v1 on v0

v1 whole, which is shorter than its diff:
```python
import functools

import jax
import jax.numpy as jnp
from jax import lax
from jax.experimental import pallas as pl
from jax.experimental.pallas import tpu as pltpu
from jax.sharding import PartitionSpec as P

MESH = pl.DeviceIdType.MESH
F32, BF16 = jnp.float32, jnp.bfloat16
NX, NY, NZ = 4, 8, 8
G = 2 * NX
TOK, ROWS, COLS, OWN, RANK = 768, 496, 1984, 248, 32
SUBS = 4
SUB = TOK // SUBS
WINDOW = 3
WORKERS = 64
HIGHEST = lax.Precision.HIGHEST


def halves(a):
    high = a.astype(BF16)
    low = (a - high.astype(F32)).astype(BF16)
    return jnp.concatenate([high, low], axis=0)


def folded(a):
    return a[:RANK] + a[RANK:]


def nn(a, b):
    return lax.dot_general(a, b, (((1,), (0,)), ((), ())), preferred_element_type=F32)


def nt(a, b):
    return lax.dot_general(a, b, (((1,), (1,)), ((), ())), preferred_element_type=F32)


def inverse_factor(gram):
    row = lax.broadcasted_iota(jnp.int32, (RANK, RANK), 0)
    col = lax.broadcasted_iota(jnp.int32, (RANK, RANK), 1)
    left, right = gram, jnp.where(row == col, 1.0, 0.0).astype(F32)
    index = lax.broadcasted_iota(jnp.int32, (RANK, 1), 0)
    for j in range(RANK):
        scale = 1.0 / jnp.sqrt(left[j : j + 1, j : j + 1])
        left_row, right_row = left[j : j + 1, :] * scale, right[j : j + 1, :] * scale
        column = left[:, j : j + 1] * scale
        below = jnp.where(index > j, column, 0.0)
        left = left - below * left_row
        right = jnp.where(row == j, right_row, right - below * right_row)
    return right


def kernel(
    x_hbm, y_hbm, e_hbm, q_hbm, out_hbm, qout,
    xv, xt, yb, ev, qv,
    tp, tr, tf, qst, qz, qall, qfull,
    pp, pr, py, pyr, pa,
    gz, gzr,
    rp, rr, ry, ryr, rz, rzr, rya, ra,
    mrg, outv, qpad, qnat,
    in_sem, out_sem, ring_s, ring_r, small_s, small_r,
):
    dp, z = lax.axis_index("dp"), lax.axis_index("shard")
    x, y, c = dp // (2 * NY), (dp // 2) % NY, dp % 2
    m = 2 * x + c

    def device(x_, y_, c_, z_):
        return ((x_ * NY + y_) * 2 + c_, z_)

    z_peers = [device(x, y, c, (z + i) % NZ) for i in range(1, NZ)]
    y_peers = [device(x, (y + i) % NY, c, z) for i in range(1, NY)]
    g_peers = [device(((m + i) % G) // 2, y, (m + i) % 2, z) for i in range(1, G)]

    loads = [
        pltpu.make_async_copy(src, dst, in_sem.at[i])
        for i, (src, dst) in enumerate([(y_hbm, yb.at[z]), (q_hbm, qv), (x_hbm, xv), (e_hbm, ev)])
    ]
    for load in loads:
        load.start()
    barrier = pltpu.get_barrier_semaphore()
    for peer in z_peers + y_peers + g_peers:
        pl.semaphore_signal(barrier, inc=1, device_id=peer, device_id_type=MESH)

    started = []

    def exchange(stage, peers, src, dst):
        copies = []
        for i, peer in enumerate(peers, 1):
            copy = pltpu.make_async_remote_copy(
                src_ref=src(i), dst_ref=dst(i), send_sem=small_s.at[stage, i - 1], recv_sem=small_r.at[stage, i - 1],
                device_id=peer, device_id_type=MESH,
            )
            copy.start()
            copies.append(copy)
        started.extend(copies)
        return copies

    def arrived(copies):
        for copy in copies:
            copy.wait_recv()

    def in_order(parts, place, count):
        total = parts[place]
        for owner in range(1, count):
            total = total + parts[(place + count - owner) % count]
        return total

    sends = [
        [(h, s) for h in range(NZ // 2) for s in range(SUBS) if h < NZ // 2 - 1 or (s < SUBS // 2) == (d == 0)]
        for d in range(2)
    ]
    ring = {}
    received, sent = set(), set()
    neighbours = (device(x, y, c, (z + 1) % NZ), device(x, y, c, (z + NZ - 1) % NZ))

    def ring_copy(d, h, s):
        owner = (z + NZ - h) % NZ if d == 0 else (z + h) % NZ
        part = yb.at[owner, pl.ds(s * SUB, SUB)]
        return pltpu.make_async_remote_copy(
            src_ref=part, dst_ref=part, send_sem=ring_s.at[d, h, s], recv_sem=ring_r.at[d, h, s],
            device_id=neighbours[d], device_id_type=MESH,
        )

    def landed(d, h, s):
        if (d, h, s) not in received:
            received.add((d, h, s))
            ring[d, h, s].wait_recv()

    def left(d, h, s):
        if (d, h, s) not in sent:
            sent.add((d, h, s))
            ring[d, h, s].wait_send()

    done = [0]

    def ticks(count):
        for _ in range(count):
            n = done[0]
            if n >= len(sends[0]):
                return
            for d in range(2):
                h, s = sends[d][n]
                if h > 0:
                    landed(d, h - 1, s)
                if n >= WINDOW:
                    left(d, *sends[d][n - WINDOW])
                ring[d, h, s] = ring_copy(d, h, s)
                ring[d, h, s].start()
            done[0] += 1

    loads[0].wait()
    loads[1].wait()
    q_own = qv[...].T
    for i in range(G):
        r, l = i % 4, i // 4
        width = min(128, OWN - 128 * l)
        if width < 128:
            qst[i] = jnp.zeros((8, 128), F32)
        qst[i, :, :width] = q_own[8 * r : 8 * r + 8, 128 * l : 128 * l + width]
    qz[z] = qst[m]
    t_own = folded(nt(halves(q_own), yb[z]))
    for k in range(NZ):
        r, l = k % 4, k // 4
        tp[k] = t_own[8 * r : 8 * r + 8, 384 * l : 384 * l + 384]
    pl.semaphore_wait(barrier, (NZ - 1) + (NY - 1) + (G - 1))

    t_sums = exchange(0, z_peers, lambda i: tp.at[(z + i) % NZ], lambda i: tr.at[i])
    q_tiles = exchange(1, z_peers, lambda i: qst.at[m], lambda i: qz.at[z])
    ticks(WINDOW)
    rp[...] = jnp.zeros(rp.shape, F32)
    pp[...] = jnp.zeros(pp.shape, F32)
    loads[2].wait()
    xt[...] = xv[...].T
    arrived(t_sums)
    total = tp[z]
    for i in range(1, NZ):
        total = total + tr[i]
    tf[z] = total
    t_parts = exchange(2, z_peers, lambda i: tf.at[z], lambda i: tf.at[z])
    arrived(q_tiles)
    qall[m] = qz[...]
    q_blocks = exchange(3, g_peers, lambda i: qz, lambda i: qall.at[m])
    ticks(2)
    arrived(q_blocks)
    for k in range(NZ):
        for i in range(G):
            r, l = i % 4, i // 4
            width = min(128, OWN - 128 * l)
            qfull[8 * r : 8 * r + 8, OWN * k + 128 * l : OWN * k + 128 * l + width] = qall[i, k, :, :width]
    loads[3].wait()
    p_error = folded(nt(halves(qfull[...]), ev[...]))
    arrived(t_parts)
    t_all = jnp.concatenate(
        [jnp.concatenate([tf[r], tf[r + 4]], axis=1) for r in range(4)], axis=0
    )
    p_own = folded(nn(halves(t_all), xv[...])) + p_error
    for i in range(G):
        x_, c_ = i // 2, i % 2
        width = min(128, ROWS - 128 * x_)
        pp[i, :, :width] = p_own[16 * c_ : 16 * c_ + 16, 128 * x_ : 128 * x_ + width]
    p_sums = exchange(4, g_peers, lambda i: pp.at[(m + i) % G], lambda i: pr.at[i])
    ticks(2)
    arrived(p_sums)
    total = pp[m]
    for i in range(1, G):
        total = total + pr[i]
    py[...] = total
    p_rows = exchange(5, y_peers, lambda i: py, lambda i: pyr.at[i])
    ticks(2)
    arrived(p_rows)
    pyr[0] = py[...]
    pa[m] = in_order(pyr, y, NY)
    p_parts = exchange(6, g_peers, lambda i: pa.at[m], lambda i: pa.at[m])
    ticks(2)
    arrived(p_parts)
    p_all = jnp.concatenate(
        [jnp.concatenate([pa[2 * x_ + c_] for x_ in range(NX)], axis=1) for c_ in range(2)], axis=0
    )[:, :ROWS]
    gram = lax.dot_general(p_all, p_all, (((1,), (1,)), ((), ())), precision=HIGHEST, preferred_element_type=F32)
    for r in range(4):
        gz[:, 32 * r : 32 * r + 32] = gram[8 * r : 8 * r + 8]
    grams = exchange(7, z_peers, lambda i: gz, lambda i: gzr.at[i])
    p_halves = halves(p_all)
    u_halves = halves(folded(nn(p_halves, xt[...])))
    r_error = folded(nn(p_halves, ev[...]))
    ticks(100)
    for d in range(2):
        for h, s in sends[d]:
            landed(d, h, s)
    for k in range(NZ):
        block = folded(nn(u_halves, yb[k])) + r_error[:, OWN * k : OWN * k + OWN]
        for c_ in range(2):
            rp[2 * (k // 2) + c_, :, 256 * (k % 2) : 256 * (k % 2) + OWN] = block[16 * c_ : 16 * c_ + 16]

    def merge(blocks):
        for k in blocks:
            span = slice(OWN * k, OWN * k + OWN)
            mrg[:, span] = nn(xt[...], yb[k]) + ev[:, span].astype(F32)

    r_sums = exchange(8, g_peers, lambda i: rp.at[(m + i) % G], lambda i: rr.at[i])
    merge(range(0, 3))
    arrived(r_sums)
    total = rp[m]
    for i in range(1, G):
        total = total + rr[i]
    for i in range(NY):
        r, l = i % 2, i // 2
        ry[i] = total[8 * r : 8 * r + 8, 128 * l : 128 * l + 128]
    r_rows = exchange(9, y_peers, lambda i: ry.at[(y + i) % NY], lambda i: ryr.at[i])
    arrived(grams)
    gzr[0] = gz[...]
    total = in_order(gzr, z, NZ)
    gram = jnp.concatenate([total[:, 32 * r : 32 * r + 32] for r in range(4)], axis=0)
    inverse = inverse_factor(gram)
    arrived(r_rows)
    total = ry[y]
    for i in range(1, NY):
        total = total + ryr[i]
    rz[...] = total
    r_tiles = exchange(10, z_peers, lambda i: rz, lambda i: rzr.at[i])
    merge(range(3, 6))
    arrived(r_tiles)
    rzr[0] = rz[...]
    rya[y] = in_order(rzr, z, NZ)
    r_back = exchange(11, y_peers, lambda i: rya.at[y], lambda i: rya.at[y])
    merge(range(6, 8))
    p_hat = lax.dot_general(inverse, p_all, (((1,), (0,)), ((), ())), precision=HIGHEST, preferred_element_type=F32)
    p_high = p_hat.astype(BF16)
    p_low = (p_hat - p_high.astype(F32)).astype(BF16)
    p_three = jnp.concatenate([p_high, p_high, p_low], axis=0).T
    arrived(r_back)
    ra[m] = rya[...]
    r_all = exchange(12, g_peers, lambda i: rya, lambda i: ra.at[m])
    arrived(r_all)
    for x_ in range(NX):
        wide = jnp.concatenate(
            [
                jnp.concatenate([ra[2 * x_ + c_, 2 * l + r] for l in range(4)], axis=1)
                for c_ in range(2)
                for r in range(2)
            ],
            axis=0,
        )
        q_wide = lax.dot_general(
            inverse, wide, (((1,), (0,)), ((), ())), precision=HIGHEST, preferred_element_type=F32
        ) * (1.0 / WORKERS)
        for j in range(2):
            k = 2 * x_ + j
            qpad[k] = q_wide[:, 256 * j : 256 * j + 256]
            qnat[:, OWN * k : OWN * k + OWN] = q_wide[:, 256 * j : 256 * j + OWN]
    q_all = qnat[...]
    q_high = q_all.astype(BF16)
    q_low = (q_all - q_high.astype(F32)).astype(BF16)
    q_three = jnp.concatenate([q_high, q_low, q_high], axis=0)
    stores = []
    for i, (first, count) in enumerate([(0, 128), (128, 128), (256, 128), (384, 112)]):
        rows = slice(first, first + count)
        outv[rows, :] = (mrg[rows, :] - nn(p_three[rows], q_three)).astype(BF16)
        store = pltpu.make_async_copy(outv.at[pl.ds(first, count)], out_hbm.at[pl.ds(first, count)], out_sem.at[i])
        store.start()
        stores.append(store)
    qout[...] = qpad[z][:, :OWN].T
    for d in range(2):
        for h, s in sends[d]:
            left(d, h, s)
    for copy in started:
        copy.wait_send()
    for store in stores:
        store.wait()


def on_device(layer_input, output_grad, error_buffer, q_start):
    any_spec = pl.BlockSpec(memory_space=pl.ANY)
    new_error, q_factor = pl.pallas_call(
        kernel,
        out_shape=(jax.ShapeDtypeStruct((ROWS, COLS), BF16), jax.ShapeDtypeStruct((OWN, RANK), F32)),
        in_specs=[any_spec] * 4,
        out_specs=(any_spec, pl.BlockSpec(memory_space=pltpu.VMEM)),
        scratch_shapes=[
            pltpu.VMEM((TOK, ROWS), BF16), pltpu.VMEM((ROWS, TOK), BF16), pltpu.VMEM((NZ, TOK, OWN), BF16),
            pltpu.VMEM((ROWS, COLS), BF16), pltpu.VMEM((OWN, RANK), F32),
            pltpu.VMEM((NZ, 8, 384), F32), pltpu.VMEM((NZ, 8, 384), F32), pltpu.VMEM((NZ, 8, 384), F32),
            pltpu.VMEM((G, 8, 128), F32), pltpu.VMEM((NZ, 8, 128), F32), pltpu.VMEM((G, NZ, 8, 128), F32),
            pltpu.VMEM((RANK, COLS), F32),
            pltpu.VMEM((G, 16, 128), F32), pltpu.VMEM((G, 16, 128), F32), pltpu.VMEM((16, 128), F32),
            pltpu.VMEM((NY, 16, 128), F32), pltpu.VMEM((G, 16, 128), F32),
            pltpu.VMEM((8, 128), F32), pltpu.VMEM((NZ, 8, 128), F32),
            pltpu.VMEM((G, 16, 512), F32), pltpu.VMEM((G, 16, 512), F32), pltpu.VMEM((NY, 8, 128), F32),
            pltpu.VMEM((NY, 8, 128), F32), pltpu.VMEM((8, 128), F32), pltpu.VMEM((NZ, 8, 128), F32),
            pltpu.VMEM((NY, 8, 128), F32), pltpu.VMEM((G, NY, 8, 128), F32),
            pltpu.VMEM((ROWS, COLS), F32), pltpu.VMEM((ROWS, COLS), BF16),
            pltpu.VMEM((NZ, RANK, 256), F32), pltpu.VMEM((RANK, COLS), F32),
            pltpu.SemaphoreType.DMA((4,)), pltpu.SemaphoreType.DMA((4,)),
            pltpu.SemaphoreType.DMA((2, NZ // 2, SUBS)), pltpu.SemaphoreType.DMA((2, NZ // 2, SUBS)),
            pltpu.SemaphoreType.DMA((13, 7)), pltpu.SemaphoreType.DMA((13, 7)),
        ],
        compiler_params=pltpu.CompilerParams(
            collective_id=0, has_side_effects=True, vmem_limit_bytes=48 * 2**20
        ),
    )(layer_input, output_grad, error_buffer[0], q_start)
    return (new_error[None], q_factor)


def solution(mesh):
    return jax.shard_map(
        on_device,
        mesh=mesh,
        in_specs=(P("dp", "shard"), P("dp", "shard"), P("dp", "shard", None), P("shard", None)),
        out_specs=(P("dp", "shard", None), P("shard", None)),
        check_vma=False,
    )
```

time: 639 us -> 91.4 us (0.14)
  waiting for transfers between devices: 300 us -> 0 us
  blocking collectives: 294 us -> 0 us
  Pallas kernels: 0 us -> 81.8 us
  matrix products: 20 us -> 0 us
  between operations: 14.1 us -> 0.67 us
  other arithmetic: 6.69 us -> 0 us
    psum x1 -> x0, waiting for transfers between devices: 271 us -> none  [on_device(): right_full = lax.psum(right_part, ('dp', 'shard'))]
    psum x2 -> x0, blocking collectives: 267 us -> none  [the longest x1 246 us: on_device(): p_sum = lax.psum(left_part, 'dp')]
    pallas_call x0 -> x1, Pallas kernels: none -> 81.8 us  [on_device(): pl.pallas_call(kernel, out_shape=(jax.ShapeDtypeStruct((ROWS, COLS), BF16...]
    all_gather x1 -> x0, waiting for transfers between devices: 29 us -> none  [on_device(): lax.all_gather(output_grad, 'shard', axis=1, tiled=True)]
    all_gather x1 -> x0, blocking collectives: 26.3 us -> none  [on_device(): start_full = lax.all_gather(q_start, 'shard', axis=0, tiled=True)]
    dot_general x5 -> x0, matrix products: 19.7 us -> none  [the longest x1 6.29 us: on_device(): approx = jnp.dot(p_hat, right_full.T, precision=lax.Precision.HIGHEST)]
    another operation x5 -> x0, other arithmetic: 6.68 us -> none  [the longest x3 3.59 us: on_device(): lower = jnp.linalg.cholesky(gram)]
    unnamed x5 -> x9, local copies, waits for them, and re-layouts: 2.06 us -> 8.68 us
  transfers between devices with their start and end apart: 2 -> 0, of which waited for: 2 -> 0; matrix products, arithmetic and copies ran while one was open for 0% -> 0% of each run, Pallas kernels for 0% -> 0%
where the time goes in v1:
time: 91.4 us; the launch traced here: 91.2 us
  Pallas kernels  81.8 us (89%)
  local copies, waits for them, and re-layouts  8.68 us (9%)
    pallas_call x1, Pallas kernels, on_device(): pl.pallas_call(kernel, out_shape=(jax.ShapeDtypeStruct((ROWS, COLS), BF16...  81.8 us
    unnamed x9, local copies, waits for them, and re-layouts  8.68 us

profile of v1, /device:TPU:1, one launch (start us, length us, event | category | flops | bytes accessed | tf_op | source)
XLA Modules:
  0.0 91.2 jit_solution(7932089684489972659)
XLA Ops:
  0.6 0.0 copy-start
  0.6 1.0 %copy.8.q_hbm = f32[248,32]{1,0:T(8,128)S(1)} copy(f32[248,32]{0,1:T(8,128)} %param.7) | data formatting | bytes 63488 | tf_op args[3]
  1.6 1.2 %copy.7.y_hbm = bf16[768,248]{1,0:T(8,128)(2,1)S(1)} copy(bf16[768,248]{0,1:T(8,128)(2,1)} %param.5) | data formatting | bytes 761856 | tf_op args[1]
  2.8 1.4 %copy.6.x_hbm = bf16[768,496]{1,0:T(8,128)(2,1)S(1)} copy(bf16[768,496]{0,1:T(8,128)(2,1)} %param.4) | data formatting | bytes 1523712 | tf_op args[0]
  4.2 0.0 copy-done
  4.2 81.8 %shard_map.59 = (bf16[496,1984]{1,0:T(8,128)(2,1)S(1)}, f32[248,32]{1,0:T(8,128)S(1)}) custom-call(bf16[768,496]{1,0:T(8,128)(2,1)S(1)} %copy.6.x_hbm, bf16[768,248]{1,0:T(8,128)(2,1)S(1)} %copy.7.y_hbm, bf16[496,1984]{1,0:T(8,128)(2,1)S(1)} %bitcast.2, f32[248,32]{1,0:T(8,128)S(1)} %copy.8.q_hbm), custom_call_target="tpu_custom_call" | custom-call | tf_op jit(solution)/shard_map/pallas_call | solution.py:316
  86.0 0.0 copy-start.1
  86.1 1.3 %copy-done.1 = bf16[496,1984]{1,0:T(8,128)(2,1)} copy-done((bf16[496,1984]{1,0:T(8,128)(2,1)}, bf16[496,1984]{1,0:T(8,128)(2,1)S(1)}, u32[]{:S(2)}) %copy-start.1) | copy-done | bytes 1968152
  87.4 0.7 copy.9
  88.1 3.1 %copy.11 = bf16[1,496,1984]{2,1,0:T(8,128)(2,1)} copy(bf16[1,496,1984]{2,1,0:T(8,128)(2,1)} %bitcast.3) | data formatting | bytes 3936256
Async XLA Ops:
  0.6 3.6 %copy-start = (bf16[1,496,1984]{2,1,0:T(8,128)(2,1)S(1)}, bf16[1,496,1984]{2,1,0:T(8,128)(2,1)}, u32[]{:S(2)}) copy-start(bf16[1,496,1984]{2,1,0:T(8,128)(2,1)} %param.6) | copy-start | bytes 5904388
  86.0 1.3 %copy-start.1 = (bf16[496,1984]{1,0:T(8,128)(2,1)}, bf16[496,1984]{1,0:T(8,128)(2,1)S(1)}, u32[]{:S(2)}) copy-start(bf16[496,1984]{1,0:T(8,128)(2,1)S(1)} %get-tuple-element.4) | copy-start | bytes 5904388

commit v2 on v1

v2 whole, which is shorter than its diff:
```python
import functools

import jax
import jax.numpy as jnp
from jax import lax
from jax.experimental import pallas as pl
from jax.experimental.pallas import tpu as pltpu
from jax.sharding import PartitionSpec as P

MESH = pl.DeviceIdType.MESH
F32, BF16 = jnp.float32, jnp.bfloat16
NX, NY, NZ = 4, 8, 8
G = 2 * NX
TOK, ROWS, COLS, OWN, RANK = 768, 496, 1984, 248, 32
SUBS = 4
SUB = TOK // SUBS
WINDOW = 3
WORKERS = 64
HIGHEST = lax.Precision.HIGHEST


def halves(a):
    high = a.astype(BF16)
    low = (a - high.astype(F32)).astype(BF16)
    return jnp.concatenate([high, low], axis=0)


def folded(a):
    return a[:RANK] + a[RANK:]


def nn(a, b):
    return lax.dot_general(a, b, (((1,), (0,)), ((), ())), preferred_element_type=F32)


def nt(a, b):
    return lax.dot_general(a, b, (((1,), (1,)), ((), ())), preferred_element_type=F32)


def thirds(a):
    high = a.astype(BF16)
    rest = a - high.astype(F32)
    middle = rest.astype(BF16)
    return high, middle, (rest - middle.astype(F32)).astype(BF16)


def product(a, b):
    a0, a1, a2 = thirds(a)
    b0, b1, b2 = thirds(b)
    return nn(jnp.concatenate([a0, a0, a0, a1, a1, a2], axis=1), jnp.concatenate([b0, b1, b2, b0, b1, b0], axis=0))


def inverse_factor(gram):
    row = lax.broadcasted_iota(jnp.int32, (RANK, RANK), 0)
    col = lax.broadcasted_iota(jnp.int32, (RANK, RANK), 1)
    left, right = gram, jnp.where(row == col, 1.0, 0.0).astype(F32)
    index = lax.broadcasted_iota(jnp.int32, (RANK, 1), 0)
    for j in range(RANK):
        scale = 1.0 / jnp.sqrt(left[j : j + 1, j : j + 1])
        left_row, right_row = left[j : j + 1, :] * scale, right[j : j + 1, :] * scale
        column = left[:, j : j + 1] * scale
        below = jnp.where(index > j, column, 0.0)
        left = left - below * left_row
        right = jnp.where(row == j, right_row, right - below * right_row)
    return right


def kernel(
    x_hbm, y_hbm, e_hbm, q_hbm,
    mrg, p_three, q_three, qout,
    xt, yt, yb, ev, qv,
    tp, tr, tf, qst, qz, qall,
    pp, pr, py, pyr, pa,
    gz, gzr,
    up, ur, uf,
    vp, vr, vs, vyr, vz, vzr, va,
    wp, wr, wy, wyr, wa, rs, ra,
    gp, rnat,
    in_sem, ring_s, ring_r, small_s, small_r,
):
    dp, z = lax.axis_index("dp"), lax.axis_index("shard")
    x, y, c = dp // (2 * NY), (dp // 2) % NY, dp % 2
    m = 2 * x + c

    def device(x_, y_, c_, z_):
        return ((x_ * NY + y_) * 2 + c_, z_)

    z_peers = [device(x, y, c, (z + i) % NZ) for i in range(1, NZ)]
    y_peers = [device(x, (y + i) % NY, c, z) for i in range(1, NY)]
    g_peers = [device(((m + i) % G) // 2, y, (m + i) % 2, z) for i in range(1, G)]

    loads = [
        pltpu.make_async_copy(src, dst, in_sem.at[i])
        for i, (src, dst) in enumerate([(y_hbm, yt), (q_hbm, qv), (x_hbm, xt), (e_hbm, ev)])
    ]
    for load in loads:
        load.start()
    barrier = pltpu.get_barrier_semaphore()
    for peer in z_peers + y_peers + g_peers:
        pl.semaphore_signal(barrier, inc=1, device_id=peer, device_id_type=MESH)

    started = []

    def exchange(stage, peers, src, dst):
        copies = {}
        for i in far_first(peers):
            copy = pltpu.make_async_remote_copy(
                src_ref=src(i), dst_ref=dst(i), send_sem=small_s.at[stage, i - 1], recv_sem=small_r.at[stage, i - 1],
                device_id=peers[i - 1], device_id_type=MESH,
            )
            copy.start()
            copies[i] = copy
        if len(started) > 1:
            for copy in started.pop(0).values():
                copy.wait_send()
        started.append(copies)
        return copies

    def far_first(peers):
        places = range(1, len(peers) + 1)
        return sorted(places, key=lambda i: -min(i, len(peers) + 1 - i))

    def arrived(copies, between=0):
        order = far_first(copies)[::-1]
        for i in order[:4]:
            copies[i].wait_recv()
        ticks(between)
        for i in order[4:]:
            copies[i].wait_recv()

    def in_order(parts, place, count):
        total = parts[place]
        for owner in range(1, count):
            total = total + parts[(place + count - owner) % count]
        return total

    def cut(a, tile):
        for i in range(G):
            r, l = i % 4, i // 4
            width = min(128, OWN - 128 * l)
            piece = a[8 * r : 8 * r + 8, 128 * l : 128 * l + width]
            tile(i)[...] = piece if width == 128 else jnp.pad(piece, ((0, 0), (0, 128 - width)))

    def uncut(tiles, out):
        for k in range(NZ):
            for i in range(G):
                r, l = i % 4, i // 4
                width = min(128, OWN - 128 * l)
                start = OWN * k + 128 * l
                out[8 * r : 8 * r + 8, start : start + width] = tiles[i, k, :, :width]

    def spread(a, parts):
        for k in range(NZ):
            r, l = k % 4, k // 4
            parts[k] = a[8 * r : 8 * r + 8, 384 * l : 384 * l + 384]

    def gathered(parts):
        return jnp.concatenate([jnp.concatenate([parts[r], parts[r + 4]], axis=1) for r in range(4)], axis=0)

    def summed(own, parts, count):
        total = own
        for i in range(1, count):
            total = total + parts[i]
        return total

    sends = [
        [(h, s) for h in range(NZ // 2) for s in range(SUBS) if h < NZ // 2 - 1 or (s < SUBS // 2) == (d == 0)]
        for d in range(2)
    ]
    ring = {}
    received, sent = set(), set()
    neighbours = (device(x, y, c, (z + 1) % NZ), device(x, y, c, (z + NZ - 1) % NZ))

    def ring_copy(d, h, s):
        owner = (z + NZ - h) % NZ if d == 0 else (z + h) % NZ
        part = yb.at[owner, pl.ds(s * SUB, SUB)]
        return pltpu.make_async_remote_copy(
            src_ref=part, dst_ref=part, send_sem=ring_s.at[d, h, s], recv_sem=ring_r.at[d, h, s],
            device_id=neighbours[d], device_id_type=MESH,
        )

    def landed(d, h, s):
        if (d, h, s) not in received:
            received.add((d, h, s))
            ring[d, h, s].wait_recv()

    def gone(d, h, s):
        if (d, h, s) not in sent:
            sent.add((d, h, s))
            ring[d, h, s].wait_send()

    done = [0]

    def ticks(count):
        for _ in range(count):
            n = done[0]
            if n >= len(sends[0]):
                return
            for d in range(2):
                h, s = sends[d][n]
                if h > 0:
                    landed(d, h - 1, s)
                if n >= WINDOW:
                    gone(d, *sends[d][n - WINDOW])
                ring[d, h, s] = ring_copy(d, h, s)
                ring[d, h, s].start()
            done[0] += 1

    loads[0].wait()
    loads[1].wait()
    q_own = qv[...]
    yb[z] = yt[...].T
    cut(q_own, lambda i: qst.at[i])
    qz[z] = qst[m]
    t_own = folded(nn(halves(q_own), yt[...]))
    spread(t_own, tp)
    pl.semaphore_wait(barrier, (NZ - 1) + (NY - 1) + (G - 1))

    q_tiles = exchange(0, z_peers, lambda i: qst.at[m], lambda i: qz.at[z])
    t_sums = exchange(1, z_peers, lambda i: tp.at[(z + i) % NZ], lambda i: tr.at[i])
    ticks(2)
    pp[...] = jnp.zeros(pp.shape, F32)
    loads[2].wait()
    arrived(q_tiles)
    qall[m] = qz[...]
    q_blocks = exchange(2, g_peers, lambda i: qz, lambda i: qall.at[m])
    arrived(t_sums)
    tf[z] = summed(tp[z], tr, NZ)
    t_parts = exchange(3, z_peers, lambda i: tf.at[z], lambda i: tf.at[z])
    ticks(2)
    loads[3].wait()
    arrived(q_blocks)
    uncut(qall, rnat)
    p_error = folded(nt(halves(rnat[...]), ev[...]))
    arrived(t_parts)
    p_own = folded(nt(halves(gathered(tf)), xt[...])) + p_error
    for i in range(G):
        x_, c_ = i // 2, i % 2
        width = min(128, ROWS - 128 * x_)
        pp[i, :, :width] = p_own[16 * c_ : 16 * c_ + 16, 128 * x_ : 128 * x_ + width]

    p_sums = exchange(4, g_peers, lambda i: pp.at[(m + i) % G], lambda i: pr.at[i])
    ticks(2)
    arrived(p_sums)
    py[...] = summed(pp[m], pr, G)
    p_rows = exchange(5, y_peers, lambda i: py, lambda i: pyr.at[i])
    ticks(2)
    arrived(p_rows)
    pyr[0] = py[...]
    pa[m] = in_order(pyr, y, NY)
    p_parts = exchange(6, g_peers, lambda i: pa.at[m], lambda i: pa.at[m])
    ticks(2)
    arrived(p_parts)
    p_all = jnp.concatenate(
        [jnp.concatenate([pa[2 * x_ + c_] for x_ in range(NX)], axis=1) for c_ in range(2)], axis=0
    )[:, :ROWS]

    p_halves = halves(p_all)
    spread(folded(nn(p_halves, xt[...])), up)
    u_sums = exchange(7, z_peers, lambda i: up.at[(z + i) % NZ], lambda i: ur.at[i])
    v_own = folded(nn(p_halves, ev[...]))
    for k in range(NZ):
        cut(v_own[:, OWN * k : OWN * k + OWN], lambda i: vp.at[i, k])
    v_sums = exchange(8, g_peers, lambda i: vp.at[(m + i) % G], lambda i: vr.at[i])
    ticks(1)
    gram = lax.dot_general(p_all, p_all, (((1,), (1,)), ((), ())), precision=HIGHEST, preferred_element_type=F32)
    for r in range(4):
        gz[:, 32 * r : 32 * r + 32] = gram[8 * r : 8 * r + 8]
    arrived(u_sums)
    uf[z] = summed(up[z], ur, NZ)
    u_parts = exchange(9, z_peers, lambda i: uf.at[z], lambda i: uf.at[z])
    grams = exchange(10, z_peers, lambda i: gz, lambda i: gzr.at[i])
    arrived(v_sums)
    vs[...] = summed(vp[m], vr, G)
    v_rows = exchange(11, y_peers, lambda i: vs.at[(y + i) % NY], lambda i: vyr.at[i])
    ticks(2)
    arrived(u_parts)
    w_own = folded(nn(halves(gathered(uf)), yb[z]))
    cut(w_own, lambda i: wp.at[i])
    w_sums = exchange(12, g_peers, lambda i: wp.at[(m + i) % G], lambda i: wr.at[i])
    arrived(v_rows)
    vz[...] = summed(vs[y], vyr, NY)
    v_tiles = exchange(13, z_peers, lambda i: vz, lambda i: vzr.at[i])
    ticks(100)
    arrived(w_sums)
    wy[...] = summed(wp[m], wr, G)
    w_rows = exchange(14, y_peers, lambda i: wy, lambda i: wyr.at[i])
    arrived(grams)
    gzr[0] = gz[...]
    total = in_order(gzr, z, NZ)
    gram = jnp.concatenate([total[:, 32 * r : 32 * r + 32] for r in range(4)], axis=0)
    inverse = inverse_factor(gram)
    arrived(w_rows)
    wyr[0] = wy[...]
    wa[z] = in_order(wyr, y, NY)
    w_tiles = exchange(15, z_peers, lambda i: wa.at[z], lambda i: wa.at[z])
    arrived(v_tiles)
    vzr[0] = vz[...]
    va[y] = in_order(vzr, z, NZ)
    v_back = exchange(16, y_peers, lambda i: va.at[y], lambda i: va.at[y])
    for d in range(2):
        for h, s in sends[d]:
            landed(d, h, s)

    def gradient(k, carry):
        gp[k] = nn(xt[...], yb[k])
        return carry

    def merge(i, carry):
        rows = pl.ds(pl.multiple_of(16 * i, 16), 16)
        for k in range(NZ):
            span = slice(OWN * k, OWN * k + OWN)
            mrg[rows, span] = gp[k, rows, :] + ev[rows, span].astype(F32)
        return carry

    lax.fori_loop(0, NZ, gradient, 0)
    arrived(w_tiles)
    arrived(v_back)
    rs[...] = wa[...] + va[...]
    ra[m] = rs[...]
    r_all = exchange(17, g_peers, lambda i: rs, lambda i: ra.at[m])
    lax.fori_loop(0, ROWS // 16, merge, 0)
    p_hat = product(inverse, p_all)
    p_high = p_hat.astype(BF16)
    p_low = (p_hat - p_high.astype(F32)).astype(BF16)
    p_three[...] = jnp.concatenate([p_high, p_high, p_low], axis=0).T
    for d in range(2):
        for h, s in sends[d]:
            gone(d, h, s)
    arrived(r_all)
    uncut(ra, rnat)
    q_all = product(inverse, rnat[...]) * (1.0 / WORKERS)
    q_high = q_all.astype(BF16)
    q_low = (q_all - q_high.astype(F32)).astype(BF16)
    q_three[...] = jnp.concatenate([q_high, q_low, q_high], axis=0)
    r_own = jnp.concatenate([jnp.concatenate([ra[r, z], ra[r + 4, z]], axis=1) for r in range(4)], axis=0)
    qout[...] = (product(inverse, r_own) * (1.0 / WORKERS))[:, :OWN]
    for copies in started:
        for copy in copies.values():
            copy.wait_send()


def finish(mrg, p_three, q_three, q_own, out_hbm, q_out, outv, out_sem):
    stores = [pltpu.make_async_copy(q_own, q_out, out_sem.at[4])]
    stores[0].start()
    for i, (first, count) in enumerate([(0, 128), (128, 128), (256, 128), (384, 112)]):
        rows = slice(first, first + count)
        outv[rows, :] = (mrg[rows, :] - nn(p_three[rows, :], q_three[...])).astype(BF16)
        store = pltpu.make_async_copy(outv.at[pl.ds(first, count)], out_hbm.at[pl.ds(first, count)], out_sem.at[i])
        store.start()
        stores.append(store)
    for store in stores:
        store.wait()


def on_device(layer_input, output_grad, error_buffer, q_start):
    hbm, vmem = pl.BlockSpec(memory_space=pltpu.HBM), pl.BlockSpec(memory_space=pltpu.VMEM)
    merged, p_three, q_three, q_own = pl.pallas_call(
        kernel,
        out_shape=(
            jax.ShapeDtypeStruct((ROWS, COLS), F32), jax.ShapeDtypeStruct((ROWS, 3 * RANK), BF16),
            jax.ShapeDtypeStruct((3 * RANK, COLS), BF16), jax.ShapeDtypeStruct((RANK, OWN), F32),
        ),
        in_specs=[hbm] * 4,
        out_specs=(vmem,) * 4,
        scratch_shapes=[
            pltpu.VMEM((ROWS, TOK), BF16), pltpu.VMEM((OWN, TOK), BF16), pltpu.VMEM((NZ, TOK, OWN), BF16),
            pltpu.VMEM((ROWS, COLS), BF16), pltpu.VMEM((RANK, OWN), F32),
            pltpu.VMEM((NZ, 8, 384), F32), pltpu.VMEM((NZ, 8, 384), F32), pltpu.VMEM((NZ, 8, 384), F32),
            pltpu.VMEM((G, 8, 128), F32), pltpu.VMEM((NZ, 8, 128), F32), pltpu.VMEM((G, NZ, 8, 128), F32),
            pltpu.VMEM((G, 16, 128), F32), pltpu.VMEM((G, 16, 128), F32), pltpu.VMEM((16, 128), F32),
            pltpu.VMEM((NY, 16, 128), F32), pltpu.VMEM((G, 16, 128), F32),
            pltpu.VMEM((8, 128), F32), pltpu.VMEM((NZ, 8, 128), F32),
            pltpu.VMEM((NZ, 8, 384), F32), pltpu.VMEM((NZ, 8, 384), F32), pltpu.VMEM((NZ, 8, 384), F32),
            pltpu.VMEM((G, NZ, 8, 128), F32), pltpu.VMEM((G, NZ, 8, 128), F32), pltpu.VMEM((NZ, 8, 128), F32),
            pltpu.VMEM((NY, 8, 128), F32), pltpu.VMEM((8, 128), F32), pltpu.VMEM((NZ, 8, 128), F32),
            pltpu.VMEM((NY, 8, 128), F32),
            pltpu.VMEM((G, 8, 128), F32), pltpu.VMEM((G, 8, 128), F32), pltpu.VMEM((8, 128), F32),
            pltpu.VMEM((NY, 8, 128), F32), pltpu.VMEM((NZ, 8, 128), F32), pltpu.VMEM((NZ, 8, 128), F32),
            pltpu.VMEM((G, NZ, 8, 128), F32),
            pltpu.VMEM((NZ, ROWS, OWN), F32), pltpu.VMEM((RANK, COLS), F32),
            pltpu.SemaphoreType.DMA((4,)),
            pltpu.SemaphoreType.DMA((2, NZ // 2, SUBS)), pltpu.SemaphoreType.DMA((2, NZ // 2, SUBS)),
            pltpu.SemaphoreType.DMA((18, 7)), pltpu.SemaphoreType.DMA((18, 7)),
        ],
        compiler_params=pltpu.CompilerParams(
            collective_id=0, has_side_effects=True, vmem_limit_bytes=40 * 2**20
        ),
    )(*(
        pltpu.with_memory_space_constraint(a, pltpu.HBM)
        for a in (layer_input.T, output_grad.T, error_buffer[0], q_start.T)
    ))
    new_error, q_factor = pl.pallas_call(
        finish,
        out_shape=(jax.ShapeDtypeStruct((ROWS, COLS), BF16), jax.ShapeDtypeStruct((RANK, OWN), F32)),
        in_specs=[vmem] * 4,
        out_specs=(hbm, hbm),
        scratch_shapes=[pltpu.VMEM((ROWS, COLS), BF16), pltpu.SemaphoreType.DMA((5,))],
        compiler_params=pltpu.CompilerParams(vmem_limit_bytes=16 * 2**20),
    )(merged, p_three, q_three, q_own)
    return (new_error[None], q_factor.T)


def solution(mesh):
    return jax.shard_map(
        on_device,
        mesh=mesh,
        in_specs=(P("dp", "shard"), P("dp", "shard"), P("dp", "shard", None), P("shard", None)),
        out_specs=(P("dp", "shard", None), P("shard", None)),
        check_vma=False,
    )
```

time: 91.4 us -> 74.2 us (0.81)
  local copies, waits for them, and re-layouts: 8.68 us -> 0 us
  Pallas kernels: 81.8 us -> 73.4 us
    unnamed x9 -> x0, local copies, waits for them, and re-layouts: 8.68 us -> none
    pallas_call x1 -> x2, Pallas kernels: 81.8 us -> 73.4 us  [the longest x1 71.8 us: on_device(): pl.pallas_call(kernel, out_shape=(jax.ShapeDtypeStruct((ROWS, COLS), F32)...]
where the time goes in v2:
time: 74.2 us; the launch traced here: 74 us
  Pallas kernels  73.4 us (99%)
    pallas_call x1, Pallas kernels, on_device(): pl.pallas_call(kernel, out_shape=(jax.ShapeDtypeStruct((ROWS, COLS), F32)...  71.8 us
    pallas_call x1, Pallas kernels, on_device(): pl.pallas_call(finish, out_shape=(jax.ShapeDtypeStruct((ROWS, COLS), BF16...  1.62 us

profile of v2, /device:TPU:1, one launch (start us, length us, event | category | flops | bytes accessed | tf_op | source)
XLA Modules:
  0.0 74.0 jit_solution(1269484769434957166)
XLA Ops:
  0.6 71.8 %shard_map.59 = (f32[496,1984]{1,0:T(8,128)S(1)}, bf16[496,96]{1,0:T(8,128)(2,1)S(1)}, bf16[96,1984]{1,0:T(8,128)(2,1)S(1)}, f32[32,248]{1,0:T(8,128)S(1)}) custom-call(bf16[496,768]{1,0:T(8,128)(2,1)} %bitcast.7, bf16[248,768]{1,0:T(8,128)(2,1)} %bitcast.8, bf16[496,1984]{1,0:T(8,128)(2,1)} %bitcast.6, f32[32,248]{1,0:T(8,128)} %bitcast.9), custom_call_target="tpu_custom_call" | custom-call | tf_op jit(solution)/shard_map/pallas_call | solution.py:358
  72.4 1.6 %shard_map.60 = (bf16[496,1984]{1,0:T(8,128)(2,1)}, f32[32,248]{1,0:T(8,128)}) custom-call(f32[496,1984]{1,0:T(8,128)S(1)} %get-tuple-element.8.mrg, bf16[496,96]{1,0:T(8,128)(2,1)S(1)} %get-tuple-element.9.p_three, bf16[96,1984]{1,0:T(8,128)(2,1)S(1)} %get-tuple-element.10.q_three, f32[32,248]{1,0:T(8,128)S(1)} %get-tuple-element.11.q_own), custom_call_target="tpu_custom_call" | custom-call | tf_op jit(solution)/shard_map/pallas_call | solution.py:393

commit v3 on v2

--- a/solution.py
+++ b/solution.py
@@ -14,7 +14,6 @@
 TOK, ROWS, COLS, OWN, RANK = 768, 496, 1984, 248, 32
 SUBS = 4
 SUB = TOK // SUBS
-WINDOW = 3
 WORKERS = 64
 HIGHEST = lax.Precision.HIGHEST
 
@@ -67,7 +66,7 @@
 
 def kernel(
     x_hbm, y_hbm, e_hbm, q_hbm,
-    mrg, p_three, q_three, qout,
+    mrg, b_three, r_three, r_own, inverse_out,
     xt, yt, yb, ev, qv,
     tp, tr, tf, qst, qz, qall,
     pp, pr, py, pyr, pa,
@@ -99,34 +98,29 @@
     for peer in z_peers + y_peers + g_peers:
         pl.semaphore_signal(barrier, inc=1, device_id=peer, device_id_type=MESH)
 
-    started = []
-
-    def exchange(stage, peers, src, dst):
-        copies = {}
-        for i in far_first(peers):
-            copy = pltpu.make_async_remote_copy(
-                src_ref=src(i), dst_ref=dst(i), send_sem=small_s.at[stage, i - 1], recv_sem=small_r.at[stage, i - 1],
-                device_id=peers[i - 1], device_id_type=MESH,
-            )
-            copy.start()
-            copies[i] = copy
-        if len(started) > 1:
-            for copy in started.pop(0).values():
-                copy.wait_send()
-        started.append(copies)
-        return copies
-
     def far_first(peers):
         places = range(1, len(peers) + 1)
         return sorted(places, key=lambda i: -min(i, len(peers) + 1 - i))
 
-    def arrived(copies, between=0):
-        order = far_first(copies)[::-1]
-        for i in order[:4]:
-            copies[i].wait_recv()
-        ticks(between)
-        for i in order[4:]:
-            copies[i].wait_recv()
+    stages = {}
+
+    def exchange(stage, peers, src, dst, buffer):
+        for i in far_first(peers):
+            pltpu.make_async_remote_copy(
+                src_ref=src(i), dst_ref=dst(i), send_sem=small_s.at[stage], recv_sem=small_r.at[stage],
+                device_id=peers[i - 1], device_id_type=MESH,
+            ).start()
+        stages[stage] = buffer.at[pl.ds(1, len(peers))]
+        return stage
+
+    def arrived(stage):
+        pltpu.make_async_copy(stages[stage], stages[stage], small_r.at[stage]).wait()
+
+    def all_sent():
+        for stage, pieces in stages.items():
+            pltpu.make_async_copy(pieces, pieces, small_s.at[stage]).wait()
+        pieces = yb.at[pl.ds(0, NZ - 1)]
+        pltpu.make_async_copy(pieces, pieces, ring_s.at[0]).wait()
 
     def in_order(parts, place, count):
         total = parts[place]
@@ -168,14 +162,14 @@
         for d in range(2)
     ]
     ring = {}
-    received, sent = set(), set()
+    received = set()
     neighbours = (device(x, y, c, (z + 1) % NZ), device(x, y, c, (z + NZ - 1) % NZ))
 
     def ring_copy(d, h, s):
         owner = (z + NZ - h) % NZ if d == 0 else (z + h) % NZ
         part = yb.at[owner, pl.ds(s * SUB, SUB)]
         return pltpu.make_async_remote_copy(
-            src_ref=part, dst_ref=part, send_sem=ring_s.at[d, h, s], recv_sem=ring_r.at[d, h, s],
+            src_ref=part, dst_ref=part, send_sem=ring_s.at[0], recv_sem=ring_r.at[d, h, s],
             device_id=neighbours[d], device_id_type=MESH,
         )
 
@@ -183,11 +177,6 @@
         if (d, h, s) not in received:
             received.add((d, h, s))
             ring[d, h, s].wait_recv()
-
-    def gone(d, h, s):
-        if (d, h, s) not in sent:
-            sent.add((d, h, s))
-            ring[d, h, s].wait_send()
 
     done = [0]
 
@@ -200,8 +189,6 @@
                 h, s = sends[d][n]
                 if h > 0:
                     landed(d, h - 1, s)
-                if n >= WINDOW:
-                    gone(d, *sends[d][n - WINDOW])
                 ring[d, h, s] = ring_copy(d, h, s)
                 ring[d, h, s].start()
             done[0] += 1
@@ -209,25 +196,25 @@
     loads[0].wait()
     loads[1].wait()
     q_own = qv[...]
-    yb[z] = yt[...].T
     cut(q_own, lambda i: qst.at[i])
     qz[z] = qst[m]
     t_own = folded(nn(halves(q_own), yt[...]))
     spread(t_own, tp)
     pl.semaphore_wait(barrier, (NZ - 1) + (NY - 1) + (G - 1))
 
-    q_tiles = exchange(0, z_peers, lambda i: qst.at[m], lambda i: qz.at[z])
-    t_sums = exchange(1, z_peers, lambda i: tp.at[(z + i) % NZ], lambda i: tr.at[i])
+    q_tiles = exchange(0, z_peers, lambda i: qst.at[m], lambda i: qz.at[z], qz)
+    t_sums = exchange(1, z_peers, lambda i: tp.at[(z + i) % NZ], lambda i: tr.at[i], tr)
+    yb[z] = yt[...].T
+    ticks(1)
+    arrived(q_tiles)
+    qall[m] = qz[...]
+    q_blocks = exchange(2, g_peers, lambda i: qz, lambda i: qall.at[m], qall)
+    arrived(t_sums)
+    tf[z] = summed(tp[z], tr, NZ)
+    t_parts = exchange(3, z_peers, lambda i: tf.at[z], lambda i: tf.at[z], tf)
     ticks(2)
     pp[...] = jnp.zeros(pp.shape, F32)
     loads[2].wait()
-    arrived(q_tiles)
-    qall[m] = qz[...]
-    q_blocks = exchange(2, g_peers, lambda i: qz, lambda i: qall.at[m])
-    arrived(t_sums)
-    tf[z] = summed(tp[z], tr, NZ)
-    t_parts = exchange(3, z_peers, lambda i: tf.at[z], lambda i: tf.at[z])
-    ticks(2)
     loads[3].wait()
     arrived(q_blocks)
     uncut(qall, rnat)
@@ -239,72 +226,82 @@
         width = min(128, ROWS - 128 * x_)
         pp[i, :, :width] = p_own[16 * c_ : 16 * c_ + 16, 128 * x_ : 128 * x_ + width]
 
-    p_sums = exchange(4, g_peers, lambda i: pp.at[(m + i) % G], lambda i: pr.at[i])
+    p_sums = exchange(4, g_peers, lambda i: pp.at[(m + i) % G], lambda i: pr.at[i], pr)
     ticks(2)
     arrived(p_sums)
     py[...] = summed(pp[m], pr, G)
-    p_rows = exchange(5, y_peers, lambda i: py, lambda i: pyr.at[i])
+    p_rows = exchange(5, y_peers, lambda i: py, lambda i: pyr.at[i], pyr)
     ticks(2)
     arrived(p_rows)
     pyr[0] = py[...]
     pa[m] = in_order(pyr, y, NY)
-    p_parts = exchange(6, g_peers, lambda i: pa.at[m], lambda i: pa.at[m])
+    p_parts = exchange(6, g_peers, lambda i: pa.at[m], lambda i: pa.at[m], pa)
     ticks(2)
     arrived(p_parts)
     p_all = jnp.concatenate(
         [jnp.concatenate([pa[2 * x_ + c_] for x_ in range(NX)], axis=1) for c_ in range(2)], axis=0
     )[:, :ROWS]
 
+    def gradients(first, count):
+        def one(i, carry):
+            owner = (z + first + i) % NZ
+            gp[owner] = nn(xt[...], yb[owner])
+            return carry
+
+        lax.fori_loop(0, count, one, 0)
+
+    def landed_steps(steps):
+        for d in range(2):
+            for h, s in sends[d]:
+                if h in steps:
+                    landed(d, h, s)
+
     p_halves = halves(p_all)
     spread(folded(nn(p_halves, xt[...])), up)
-    u_sums = exchange(7, z_peers, lambda i: up.at[(z + i) % NZ], lambda i: ur.at[i])
+    u_sums = exchange(7, z_peers, lambda i: up.at[(z + i) % NZ], lambda i: ur.at[i], ur)
     v_own = folded(nn(p_halves, ev[...]))
     for k in range(NZ):
         cut(v_own[:, OWN * k : OWN * k + OWN], lambda i: vp.at[i, k])
-    v_sums = exchange(8, g_peers, lambda i: vp.at[(m + i) % G], lambda i: vr.at[i])
-    ticks(1)
+    v_sums = exchange(8, g_peers, lambda i: vp.at[(m + i) % G], lambda i: vr.at[i], vr)
+    ticks(2)
+    arrived(u_sums)
+    uf[z] = summed(up[z], ur, NZ)
+    u_parts = exchange(9, z_peers, lambda i: uf.at[z], lambda i: uf.at[z], uf)
     gram = lax.dot_general(p_all, p_all, (((1,), (1,)), ((), ())), precision=HIGHEST, preferred_element_type=F32)
     for r in range(4):
         gz[:, 32 * r : 32 * r + 32] = gram[8 * r : 8 * r + 8]
-    arrived(u_sums)
-    uf[z] = summed(up[z], ur, NZ)
-    u_parts = exchange(9, z_peers, lambda i: uf.at[z], lambda i: uf.at[z])
-    grams = exchange(10, z_peers, lambda i: gz, lambda i: gzr.at[i])
+    grams = exchange(10, z_peers, lambda i: gz, lambda i: gzr.at[i], gzr)
     arrived(v_sums)
     vs[...] = summed(vp[m], vr, G)
-    v_rows = exchange(11, y_peers, lambda i: vs.at[(y + i) % NY], lambda i: vyr.at[i])
+    v_rows = exchange(11, y_peers, lambda i: vs.at[(y + i) % NY], lambda i: vyr.at[i], vyr)
     ticks(2)
     arrived(u_parts)
     w_own = folded(nn(halves(gathered(uf)), yb[z]))
     cut(w_own, lambda i: wp.at[i])
-    w_sums = exchange(12, g_peers, lambda i: wp.at[(m + i) % G], lambda i: wr.at[i])
+    w_sums = exchange(12, g_peers, lambda i: wp.at[(m + i) % G], lambda i: wr.at[i], wr)
     arrived(v_rows)
     vz[...] = summed(vs[y], vyr, NY)
-    v_tiles = exchange(13, z_peers, lambda i: vz, lambda i: vzr.at[i])
+    v_tiles = exchange(13, z_peers, lambda i: vz, lambda i: vzr.at[i], vzr)
     ticks(100)
-    arrived(w_sums)
-    wy[...] = summed(wp[m], wr, G)
-    w_rows = exchange(14, y_peers, lambda i: wy, lambda i: wyr.at[i])
     arrived(grams)
     gzr[0] = gz[...]
     total = in_order(gzr, z, NZ)
     gram = jnp.concatenate([total[:, 32 * r : 32 * r + 32] for r in range(4)], axis=0)
     inverse = inverse_factor(gram)
+    arrived(w_sums)
+    wy[...] = summed(wp[m], wr, G)
+    w_rows = exchange(14, y_peers, lambda i: wy, lambda i: wyr.at[i], wyr)
+    landed_steps((0, 1))
+    gradients(6, 5)
     arrived(w_rows)
     wyr[0] = wy[...]
     wa[z] = in_order(wyr, y, NY)
-    w_tiles = exchange(15, z_peers, lambda i: wa.at[z], lambda i: wa.at[z])
+    w_tiles = exchange(15, z_peers, lambda i: wa.at[z], lambda i: wa.at[z], wa)
     arrived(v_tiles)
     vzr[0] = vz[...]
     va[y] = in_order(vzr, z, NZ)
-    v_back = exchange(16, y_peers, lambda i: va.at[y], lambda i: va.at[y])
-    for d in range(2):
-        for h, s in sends[d]:
-            landed(d, h, s)
-
-    def gradient(k, carry):
-        gp[k] = nn(xt[...], yb[k])
-        return carry
+    v_back = exchange(16, y_peers, lambda i: va.at[y], lambda i: va.at[y], va)
+    landed_steps((2, 3))
 
     def merge(i, carry):
         rows = pl.ds(pl.multiple_of(16 * i, 16), 16)
@@ -313,56 +310,55 @@
             mrg[rows, span] = gp[k, rows, :] + ev[rows, span].astype(F32)
         return carry
 
-    lax.fori_loop(0, NZ, gradient, 0)
+    gradients(3, 3)
     arrived(w_tiles)
     arrived(v_back)
     rs[...] = wa[...] + va[...]
     ra[m] = rs[...]
-    r_all = exchange(17, g_peers, lambda i: rs, lambda i: ra.at[m])
+    r_all = exchange(17, g_peers, lambda i: rs, lambda i: ra.at[m], ra)
     lax.fori_loop(0, ROWS // 16, merge, 0)
     p_hat = product(inverse, p_all)
-    p_high = p_hat.astype(BF16)
-    p_low = (p_hat - p_high.astype(F32)).astype(BF16)
-    p_three[...] = jnp.concatenate([p_high, p_high, p_low], axis=0).T
-    for d in range(2):
-        for h, s in sends[d]:
-            gone(d, h, s)
+    b = product(inverse.T, p_hat) * (1.0 / WORKERS)
+    b_high = b.astype(BF16)
+    b_low = (b - b_high.astype(F32)).astype(BF16)
+    b_three[...] = jnp.concatenate([b_high, b_high, b_low], axis=0).T
+    inverse_out[...] = inverse
     arrived(r_all)
     uncut(ra, rnat)
-    q_all = product(inverse, rnat[...]) * (1.0 / WORKERS)
-    q_high = q_all.astype(BF16)
-    q_low = (q_all - q_high.astype(F32)).astype(BF16)
-    q_three[...] = jnp.concatenate([q_high, q_low, q_high], axis=0)
-    r_own = jnp.concatenate([jnp.concatenate([ra[r, z], ra[r + 4, z]], axis=1) for r in range(4)], axis=0)
-    qout[...] = (product(inverse, r_own) * (1.0 / WORKERS))[:, :OWN]
-    for copies in started:
-        for copy in copies.values():
-            copy.wait_send()
-
-
-def finish(mrg, p_three, q_three, q_own, out_hbm, q_out, outv, out_sem):
-    stores = [pltpu.make_async_copy(q_own, q_out, out_sem.at[4])]
-    stores[0].start()
+    r_all = rnat[...]
+    r_high = r_all.astype(BF16)
+    r_low = (r_all - r_high.astype(F32)).astype(BF16)
+    r_three[...] = jnp.concatenate([r_high, r_low, r_high], axis=0)
+    r_own[...] = jnp.concatenate([jnp.concatenate([ra[r, z], ra[r + 4, z]], axis=1) for r in range(4)], axis=0)
+    all_sent()
+
+
+def finish(mrg, b_three, r_three, r_own, inverse, out_hbm, q_out, outv, q_own, out_sem):
+    stores = []
     for i, (first, count) in enumerate([(0, 128), (128, 128), (256, 128), (384, 112)]):
         rows = slice(first, first + count)
-        outv[rows, :] = (mrg[rows, :] - nn(p_three[rows, :], q_three[...])).astype(BF16)
+        outv[rows, :] = (mrg[rows, :] - nn(b_three[rows, :], r_three[...])).astype(BF16)
         store = pltpu.make_async_copy(outv.at[pl.ds(first, count)], out_hbm.at[pl.ds(first, count)], out_sem.at[i])
         store.start()
         stores.append(store)
+    q_own[...] = (product(inverse[...], r_own[...]) * (1.0 / WORKERS))[:, :OWN]
+    stores.append(pltpu.make_async_copy(q_own, q_out, out_sem.at[4]))
+    stores[-1].start()
     for store in stores:
         store.wait()
 
 
 def on_device(layer_input, output_grad, error_buffer, q_start):
     hbm, vmem = pl.BlockSpec(memory_space=pltpu.HBM), pl.BlockSpec(memory_space=pltpu.VMEM)
-    merged, p_three, q_three, q_own = pl.pallas_call(
+    merged, b_three, r_three, r_own, inverse = pl.pallas_call(
         kernel,
         out_shape=(
             jax.ShapeDtypeStruct((ROWS, COLS), F32), jax.ShapeDtypeStruct((ROWS, 3 * RANK), BF16),
-            jax.ShapeDtypeStruct((3 * RANK, COLS), BF16), jax.ShapeDtypeStruct((RANK, OWN), F32),
+            jax.ShapeDtypeStruct((3 * RANK, COLS), BF16), jax.ShapeDtypeStruct((RANK, 256), F32),
+            jax.ShapeDtypeStruct((RANK, RANK), F32),
         ),
         in_specs=[hbm] * 4,
-        out_specs=(vmem,) * 4,
+        out_specs=(vmem,) * 5,
         scratch_shapes=[
             pltpu.VMEM((ROWS, TOK), BF16), pltpu.VMEM((OWN, TOK), BF16), pltpu.VMEM((NZ, TOK, OWN), BF16),
             pltpu.VMEM((ROWS, COLS), BF16), pltpu.VMEM((RANK, OWN), F32),
@@ -380,8 +376,8 @@
             pltpu.VMEM((G, NZ, 8, 128), F32),
             pltpu.VMEM((NZ, ROWS, OWN), F32), pltpu.VMEM((RANK, COLS), F32),
             pltpu.SemaphoreType.DMA((4,)),
-            pltpu.SemaphoreType.DMA((2, NZ // 2, SUBS)), pltpu.SemaphoreType.DMA((2, NZ // 2, SUBS)),
-            pltpu.SemaphoreType.DMA((18, 7)), pltpu.SemaphoreType.DMA((18, 7)),
+            pltpu.SemaphoreType.DMA((1,)), pltpu.SemaphoreType.DMA((2, NZ // 2, SUBS)),
+            pltpu.SemaphoreType.DMA((18,)), pltpu.SemaphoreType.DMA((18,)),
         ],
         compiler_params=pltpu.CompilerParams(
             collective_id=0, has_side_effects=True, vmem_limit_bytes=40 * 2**20
@@ -393,11 +389,11 @@
     new_error, q_factor = pl.pallas_call(
         finish,
         out_shape=(jax.ShapeDtypeStruct((ROWS, COLS), BF16), jax.ShapeDtypeStruct((RANK, OWN), F32)),
-        in_specs=[vmem] * 4,
+        in_specs=[vmem] * 5,
         out_specs=(hbm, hbm),
-        scratch_shapes=[pltpu.VMEM((ROWS, COLS), BF16), pltpu.SemaphoreType.DMA((5,))],
+        scratch_shapes=[pltpu.VMEM((ROWS, COLS), BF16), pltpu.VMEM((RANK, OWN), F32), pltpu.SemaphoreType.DMA((5,))],
         compiler_params=pltpu.CompilerParams(vmem_limit_bytes=16 * 2**20),
-    )(merged, p_three, q_three, q_own)
+    )(merged, b_three, r_three, r_own, inverse)
     return (new_error[None], q_factor.T)
 
 

time: 74.2 us -> 72.3 us (0.974)
  Pallas kernels: 73.4 us -> 71.6 us
    pallas_call x1, Pallas kernels: 71.8 us -> 70 us  [on_device(): pl.pallas_call(kernel, out_shape=(jax.ShapeDtypeStruct((ROWS, COLS), F32)...]
where the time goes in v3:
time: 72.3 us; the launch traced here: 72.2 us
  Pallas kernels  71.6 us (99%)
    pallas_call x1, Pallas kernels, on_device(): pl.pallas_call(kernel, out_shape=(jax.ShapeDtypeStruct((ROWS, COLS), F32)...  70 us
    pallas_call x1, Pallas kernels, on_device(): pl.pallas_call(finish, out_shape=(jax.ShapeDtypeStruct((ROWS, COLS), BF16...  1.63 us

profile of v3, /device:TPU:1, one launch (start us, length us, event | category | flops | bytes accessed | tf_op | source)
XLA Modules:
  0.0 72.2 jit_solution(3198565009743173275)
XLA Ops:
  0.6 70.0 %shard_map.59 = (f32[496,1984]{1,0:T(8,128)S(1)}, bf16[496,96]{1,0:T(8,128)(2,1)S(1)}, bf16[96,1984]{1,0:T(8,128)(2,1)S(1)}, f32[32,256]{1,0:T(8,128)S(1)}, f32[32,32]{1,0:T(8,128)S(1)}) custom-call(bf16[496,768]{1,0:T(8,128)(2,1)} %bitcast.7, bf16[248,768]{1,0:T(8,128)(2,1)} %bitcast.8, bf16[496,1984]{1,0:T(8,128)(2,1)} %bitcast.6, f32[32,248]{1,0:T(8,128)} %bitcast.9), custom_call_target="tpu_custom_call" | custom-call | tf_op jit(solution)/shard_map/pallas_call | solution.py:353
  70.6 1.6 %shard_map.60 = (bf16[496,1984]{1,0:T(8,128)(2,1)}, f32[32,248]{1,0:T(8,128)}) custom-call(f32[496,1984]{1,0:T(8,128)S(1)} %get-tuple-element.9.mrg, bf16[496,96]{1,0:T(8,128)(2,1)S(1)} %get-tuple-element.10.b_three, bf16[96,1984]{1,0:T(8,128)(2,1)S(1)} %get-tuple-element.11.r_three, f32[32,256]{1,0:T(8,128)S(1)} %get-tuple-element.12.r_own, ...), custom_call_target="tpu_custom_call" | custom-call | tf_op jit(solution)/shard_map/pallas_call | solution.py:389

commit v4 on v3

--- a/solution.py
+++ b/solution.py
@@ -92,8 +92,8 @@
         pltpu.make_async_copy(src, dst, in_sem.at[i])
         for i, (src, dst) in enumerate([(y_hbm, yt), (q_hbm, qv), (x_hbm, xt), (e_hbm, ev)])
     ]
-    for load in loads:
-        load.start()
+    loads[1].start()
+    loads[0].start()
     barrier = pltpu.get_barrier_semaphore()
     for peer in z_peers + y_peers + g_peers:
         pl.semaphore_signal(barrier, inc=1, device_id=peer, device_id_type=MESH)
@@ -193,16 +193,16 @@
                 ring[d, h, s].start()
             done[0] += 1
 
-    loads[0].wait()
     loads[1].wait()
     q_own = qv[...]
     cut(q_own, lambda i: qst.at[i])
     qz[z] = qst[m]
-    t_own = folded(nn(halves(q_own), yt[...]))
-    spread(t_own, tp)
     pl.semaphore_wait(barrier, (NZ - 1) + (NY - 1) + (G - 1))
-
     q_tiles = exchange(0, z_peers, lambda i: qst.at[m], lambda i: qz.at[z], qz)
+    loads[0].wait()
+    loads[2].start()
+    loads[3].start()
+    spread(folded(nn(halves(q_own), yt[...])), tp)
     t_sums = exchange(1, z_peers, lambda i: tp.at[(z + i) % NZ], lambda i: tr.at[i], tr)
     yb[z] = yt[...].T
     ticks(1)
@@ -307,22 +307,23 @@
         rows = pl.ds(pl.multiple_of(16 * i, 16), 16)
         for k in range(NZ):
             span = slice(OWN * k, OWN * k + OWN)
-            mrg[rows, span] = gp[k, rows, :] + ev[rows, span].astype(F32)
+            mrg[rows, span] = gp[k, rows, :]
+        mrg[rows, :] = mrg[rows, :] + ev[rows, :].astype(F32)
         return carry
 
     gradients(3, 3)
+    p_hat = product(inverse, p_all)
+    b = product(inverse.T, p_hat) * (1.0 / WORKERS)
+    b_high = b.astype(BF16)
+    b_low = (b - b_high.astype(F32)).astype(BF16)
+    b_three[...] = jnp.concatenate([b_high, b_high, b_low], axis=0).T
+    inverse_out[...] = inverse
     arrived(w_tiles)
     arrived(v_back)
     rs[...] = wa[...] + va[...]
     ra[m] = rs[...]
     r_all = exchange(17, g_peers, lambda i: rs, lambda i: ra.at[m], ra)
     lax.fori_loop(0, ROWS // 16, merge, 0)
-    p_hat = product(inverse, p_all)
-    b = product(inverse.T, p_hat) * (1.0 / WORKERS)
-    b_high = b.astype(BF16)
-    b_low = (b - b_high.astype(F32)).astype(BF16)
-    b_three[...] = jnp.concatenate([b_high, b_high, b_low], axis=0).T
-    inverse_out[...] = inverse
     arrived(r_all)
     uncut(ra, rnat)
     r_all = rnat[...]

time: 72.3 us -> 72.3 us (level)
  no operation moved by 1% of the time
where the time goes in v4:
time: 72.3 us; the launch traced here: 72.1 us
  Pallas kernels  71.5 us (99%)
    pallas_call x1, Pallas kernels, on_device(): pl.pallas_call(kernel, out_shape=(jax.ShapeDtypeStruct((ROWS, COLS), F32)...  69.9 us
    pallas_call x1, Pallas kernels, on_device(): pl.pallas_call(finish, out_shape=(jax.ShapeDtypeStruct((ROWS, COLS), BF16...  1.62 us

profile of v4, /device:TPU:1, one launch (start us, length us, event | category | flops | bytes accessed | tf_op | source)
XLA Modules:
  0.0 72.1 jit_solution(9878175661905799347)
XLA Ops:
  0.6 69.9 %shard_map.59 = (f32[496,1984]{1,0:T(8,128)S(1)}, bf16[496,96]{1,0:T(8,128)(2,1)S(1)}, bf16[96,1984]{1,0:T(8,128)(2,1)S(1)}, f32[32,256]{1,0:T(8,128)S(1)}, f32[32,32]{1,0:T(8,128)S(1)}) custom-call(bf16[496,768]{1,0:T(8,128)(2,1)} %bitcast.7, bf16[248,768]{1,0:T(8,128)(2,1)} %bitcast.8, bf16[496,1984]{1,0:T(8,128)(2,1)} %bitcast.6, f32[32,248]{1,0:T(8,128)} %bitcast.9), custom_call_target="tpu_custom_call" | custom-call | tf_op jit(solution)/shard_map/pallas_call | solution.py:354
  70.5 1.6 %shard_map.60 = (bf16[496,1984]{1,0:T(8,128)(2,1)}, f32[32,248]{1,0:T(8,128)}) custom-call(f32[496,1984]{1,0:T(8,128)S(1)} %get-tuple-element.9.mrg, bf16[496,96]{1,0:T(8,128)(2,1)S(1)} %get-tuple-element.10.b_three, bf16[96,1984]{1,0:T(8,128)(2,1)S(1)} %get-tuple-element.11.r_three, f32[32,256]{1,0:T(8,128)S(1)} %get-tuple-element.12.r_own, ...), custom_call_target="tpu_custom_call" | custom-call | tf_op jit(solution)/shard_map/pallas_call | solution.py:390

commit v5 on v3

--- a/solution.py
+++ b/solution.py
@@ -12,7 +12,7 @@
 NX, NY, NZ = 4, 8, 8
 G = 2 * NX
 TOK, ROWS, COLS, OWN, RANK = 768, 496, 1984, 248, 32
-SUBS = 4
+SUBS = 2
 SUB = TOK // SUBS
 WORKERS = 64
 HIGHEST = lax.Precision.HIGHEST
@@ -212,7 +212,7 @@
     arrived(t_sums)
     tf[z] = summed(tp[z], tr, NZ)
     t_parts = exchange(3, z_peers, lambda i: tf.at[z], lambda i: tf.at[z], tf)
-    ticks(2)
+    ticks(1)
     pp[...] = jnp.zeros(pp.shape, F32)
     loads[2].wait()
     loads[3].wait()
@@ -227,16 +227,16 @@
         pp[i, :, :width] = p_own[16 * c_ : 16 * c_ + 16, 128 * x_ : 128 * x_ + width]
 
     p_sums = exchange(4, g_peers, lambda i: pp.at[(m + i) % G], lambda i: pr.at[i], pr)
-    ticks(2)
+    ticks(1)
     arrived(p_sums)
     py[...] = summed(pp[m], pr, G)
     p_rows = exchange(5, y_peers, lambda i: py, lambda i: pyr.at[i], pyr)
-    ticks(2)
+    ticks(1)
     arrived(p_rows)
     pyr[0] = py[...]
     pa[m] = in_order(pyr, y, NY)
     p_parts = exchange(6, g_peers, lambda i: pa.at[m], lambda i: pa.at[m], pa)
-    ticks(2)
+    ticks(1)
     arrived(p_parts)
     p_all = jnp.concatenate(
         [jnp.concatenate([pa[2 * x_ + c_] for x_ in range(NX)], axis=1) for c_ in range(2)], axis=0
@@ -263,7 +263,7 @@
     for k in range(NZ):
         cut(v_own[:, OWN * k : OWN * k + OWN], lambda i: vp.at[i, k])
     v_sums = exchange(8, g_peers, lambda i: vp.at[(m + i) % G], lambda i: vr.at[i], vr)
-    ticks(2)
+    ticks(1)
     arrived(u_sums)
     uf[z] = summed(up[z], ur, NZ)
     u_parts = exchange(9, z_peers, lambda i: uf.at[z], lambda i: uf.at[z], uf)
@@ -274,7 +274,7 @@
     arrived(v_sums)
     vs[...] = summed(vp[m], vr, G)
     v_rows = exchange(11, y_peers, lambda i: vs.at[(y + i) % NY], lambda i: vyr.at[i], vyr)
-    ticks(2)
+    ticks(1)
     arrived(u_parts)
     w_own = folded(nn(halves(gathered(uf)), yb[z]))
     cut(w_own, lambda i: wp.at[i])

time: 72.3 us -> 73.6 us (1.018)
  Pallas kernels: 71.6 us -> 72.9 us
    pallas_call x1, Pallas kernels: 70 us -> 71.2 us  [on_device(): pl.pallas_call(kernel, out_shape=(jax.ShapeDtypeStruct((ROWS, COLS), F32)...]
where the time goes in v5:
time: 73.6 us; the launch traced here: 73.5 us
  Pallas kernels  72.9 us (99%)
    pallas_call x1, Pallas kernels, on_device(): pl.pallas_call(kernel, out_shape=(jax.ShapeDtypeStruct((ROWS, COLS), F32)...  71.2 us
    pallas_call x1, Pallas kernels, on_device(): pl.pallas_call(finish, out_shape=(jax.ShapeDtypeStruct((ROWS, COLS), BF16...  1.63 us

profile of v5, /device:TPU:1, one launch (start us, length us, event | category | flops | bytes accessed | tf_op | source)
XLA Modules:
  0.0 73.5 jit_solution(13689094781164213434)
XLA Ops:
  0.6 71.2 %shard_map.59 = (f32[496,1984]{1,0:T(8,128)S(1)}, bf16[496,96]{1,0:T(8,128)(2,1)S(1)}, bf16[96,1984]{1,0:T(8,128)(2,1)S(1)}, f32[32,256]{1,0:T(8,128)S(1)}, f32[32,32]{1,0:T(8,128)S(1)}) custom-call(bf16[496,768]{1,0:T(8,128)(2,1)} %bitcast.7, bf16[248,768]{1,0:T(8,128)(2,1)} %bitcast.8, bf16[496,1984]{1,0:T(8,128)(2,1)} %bitcast.6, f32[32,248]{1,0:T(8,128)} %bitcast.9), custom_call_target="tpu_custom_call" | custom-call | tf_op jit(solution)/shard_map/pallas_call | solution.py:353
  71.9 1.6 %shard_map.60 = (bf16[496,1984]{1,0:T(8,128)(2,1)}, f32[32,248]{1,0:T(8,128)}) custom-call(f32[496,1984]{1,0:T(8,128)S(1)} %get-tuple-element.9.mrg, bf16[496,96]{1,0:T(8,128)(2,1)S(1)} %get-tuple-element.10.b_three, bf16[96,1984]{1,0:T(8,128)(2,1)S(1)} %get-tuple-element.11.r_three, f32[32,256]{1,0:T(8,128)S(1)} %get-tuple-element.12.r_own, ...), custom_call_target="tpu_custom_call" | custom-call | tf_op jit(solution)/shard_map/pallas_call | solution.py:389
